TPU v7x, 32 devices: a whole 2x2x4 slice. The times are simulated.
32 devices in a mesh: seq: 8 (over y, x, core), tp: 4 (over z).
Axes of the slice: x: 2, y: 2, z: 4, core: 2. Of those that a mesh axis runs over, the one named last changes fastest.
Arguments:
- residual: bfloat16 [4096, 2048], P('seq', 'tp'), may hold values from -6 to 6
- norm_gain: float32 [2048], replicated, may hold values from 0.3 to 3
- query_weight: bfloat16 [2048, 1024], P(None, 'tp'), as said below
- key_weight: bfloat16 [2048, 1024], P(None, 'tp'), as said below
- value_weight: bfloat16 [2048, 1024], P(None, 'tp'), may hold values from -0.375 to 0.375
- out_weight: bfloat16 [1024, 2048], P('tp'), may hold values from -0.1875 to 0.1875
- segment_start: int32 [4096], P('seq'), may hold values from 0 to 3968, as said below
- token_valid: int32 [4096], P('seq'), may hold values from 0 to 1, as said below
- page_slot: int32 [32], P('seq'), may hold values from 4 to 63, as said below
Outputs:
- hidden: bfloat16 [4096, 2048], P('seq', 'tp')
- cache: bfloat16 [64, 128, 2048], P('seq', None, 'tp')
Inputs may be any that keep to these rules, and one draw needn't show every extreme that they name: `segment_start`: prompts start at multiples of 128 and are contiguous; each holds at most 2048 tokens and one holds exactly 2048. `token_valid`: zeros form a tail of the last page of a prompt; the first token of every prompt is 1. No two pages share a cache page; page_slot // 8 is the device that holds the page's tokens, or the next device when that one holds tokens of the same prompt. `query_weight`: independent entries whose scale falls as the inverse square root of 2048. `key_weight`: independent entries whose scale falls as the inverse square root of 2048.
All inputs are finite; a program needn't handle non-finite values.
Results may differ from a plain program's by a relative error of at most 0.02.
The roundings to bfloat16 on the way count: a program that leaves them out, or rounds other values in their place, can miss the bound.
Values may be sent and summed in bfloat16 or wider, within the bound.
A program may use at most 128 MiB of HBM per device.

v0:
```python
import jax
import jax.numpy as jnp
from jax import lax
from jax.sharding import PartitionSpec as P

HD = 64
PAGE = 128
SPAN = 16


THETA = 130000.0
EPS = 1e-05


def passed_along(x, axis, by):
    count = lax.axis_size(axis)
    pairs = [(i, i + by) for i in range(count) if 0 <= i + by < count]
    return lax.ppermute(x, axis, pairs)


def rotate(inputs, positions):
    half_dim = inputs.shape[-1] // 2
    frequency = THETA ** (-2.0 * jnp.arange(half_dim, dtype=jnp.float32) / inputs.shape[-1])
    angles = positions.astype(jnp.float32)[:, None] * frequency[None, :]
    cosine = jnp.cos(angles)[:, None, :]
    sine_part = jnp.sin(angles)[:, None, :]
    front_half = inputs[..., :half_dim]
    back_half = inputs[..., half_dim:]
    return jnp.concatenate(
        [front_half * cosine - back_half * sine_part, back_half * cosine + front_half * sine_part],
        axis=-1,
    )


def body(
    residual,
    norm_gain,
    query_weight,
    key_weight,
    value_weight,
    out_weight,
    segment_start,
    token_valid,
    page_slot,
):
    row_count = residual.shape[0]
    local_heads = query_weight.shape[1] // HD
    gathered = lax.all_gather(residual, "tp", axis=1, tiled=True)
    widened = gathered.astype(jnp.float32)
    mean_sq = jnp.mean(widened * widened, axis=1, keepdims=True)
    normed = (widened * lax.rsqrt(mean_sq + EPS) * norm_gain[None, :]).astype(jnp.bfloat16)
    seq_rank = lax.axis_index("seq")
    first_row = seq_rank * row_count
    places = first_row + jnp.arange(row_count, dtype=jnp.int32)
    offsets = places - segment_start
    queries = jnp.dot(normed, query_weight, preferred_element_type=jnp.float32).reshape(
        row_count, local_heads, HD
    )
    queries = rotate(queries, offsets).astype(jnp.bfloat16)
    key_rot = jnp.dot(normed, key_weight, preferred_element_type=jnp.float32).reshape(
        row_count, local_heads, HD
    )
    key_rot = rotate(key_rot, offsets).astype(jnp.bfloat16)
    values = (
        jnp.dot(normed, value_weight, preferred_element_type=jnp.float32)
        .reshape(row_count, local_heads, HD)
        .astype(jnp.bfloat16)
    )
    packed = jnp.concatenate([key_rot[:, :, None, :], values[:, :, None, :]], axis=2).reshape(
        row_count, local_heads * 2 * HD
    )
    packed = jnp.where(token_valid[:, None] > 0, packed, jnp.zeros_like(packed))
    key_group = jnp.where(token_valid > 0, segment_start, -1)
    in_page = jnp.arange(row_count, dtype=jnp.int32) % PAGE
    page_rows = jnp.repeat(page_slot, PAGE) * PAGE + in_page
    slot_count = 2 * page_slot.shape[0]
    cache_size = slot_count * PAGE
    base_row = seq_rank * cache_size
    score_scale = HD ** (-0.5)

    def attend_block(running, incoming, allowed):
        row_max, norm_sum, weighted = running
        key_value = incoming[0].reshape(incoming[0].shape[0], local_heads, 2, HD)
        scores = (
            jnp.einsum(
                "qhd,khd->hqk", queries, key_value[:, :, 0, :], preferred_element_type=jnp.float32
            )
            * score_scale
        )
        block_max = jnp.max(jnp.where(allowed[None], scores, -1e30), axis=2)
        new_max = jnp.maximum(row_max, block_max)
        weights = jnp.where(allowed[None], jnp.exp(scores - new_max[:, :, None]), 0.0)
        shrink = jnp.exp(row_max - new_max)
        norm_sum = norm_sum * shrink + jnp.sum(weights, axis=2)
        update = jnp.einsum(
            "hqk,khd->qhd",
            weights.astype(jnp.bfloat16),
            key_value[:, :, 1, :],
            preferred_element_type=jnp.float32,
        )
        weighted = weighted * jnp.transpose(shrink)[:, :, None] + update
        return (new_max, norm_sum, weighted)

    def absorb(carried, incoming, begin_row):
        row_max, norm_sum, weighted, cache_rows = carried
        key_count = incoming[0].shape[0]
        key_places = begin_row + jnp.arange(key_count, dtype=jnp.int32)
        allowed = (
            (incoming[1][None, :] == segment_start[:, None])
            & (key_places[None, :] <= places[:, None])
            & (key_places[None, :] >= 0)
        )
        local_dest = incoming[2] - base_row
        in_range = (local_dest >= 0) & (local_dest < cache_size) & (key_places >= 0)
        target = jnp.where(in_range, local_dest, cache_size)
        cache_rows = cache_rows.at[target].set(incoming[0], mode="drop")
        running = attend_block((row_max, norm_sum, weighted), incoming, allowed)
        return (running[0], running[1], running[2], cache_rows)

    initial = (
        jnp.full((local_heads, row_count), -1e30, jnp.float32),
        jnp.zeros((local_heads, row_count), jnp.float32),
        jnp.zeros((row_count, local_heads, HD), jnp.float32),
        jnp.zeros((cache_size, local_heads * 2 * HD), jnp.bfloat16),
    )
    own_block = (packed, key_group, page_rows)
    carried = absorb(initial, own_block, first_row)
    reach_dev = min(SPAN, lax.axis_size("seq") // 2)

    def advance(step_index, carry_in):
        moving, carry_state = carry_in
        moving = passed_along((moving[0], moving[1], moving[2]), "seq", 1)
        carry_state = absorb(carry_state, moving, first_row - (step_index + 1) * row_count)
        return (moving, carry_state)

    moving, carried = lax.fori_loop(0, reach_dev, advance, (own_block, carried))
    row_max, norm_sum, weighted, cache_rows = carried
    attended = (
        (weighted / jnp.transpose(norm_sum)[:, :, None])
        .astype(jnp.bfloat16)
        .reshape(row_count, local_heads * HD)
    )
    projected = jnp.dot(attended, out_weight, preferred_element_type=jnp.float32)
    summed = lax.psum_scatter(
        projected.astype(jnp.bfloat16), "tp", scatter_dimension=1, tiled=True
    ).astype(jnp.float32)
    hidden = (residual.astype(jnp.float32) + summed).astype(jnp.bfloat16)
    return (hidden, cache_rows.reshape(slot_count, PAGE, local_heads * 2 * HD))


def solution(mesh):
    return jax.shard_map(
        body,
        mesh=mesh,
        in_specs=(
            P("seq", "tp"),
            P(),
            P(None, "tp"),
            P(None, "tp"),
            P(None, "tp"),
            P("tp", None),
            P("seq"),
            P("seq"),
            P("seq"),
        ),
        out_specs=(P("seq", "tp"), P("seq", None, "tp")),
        check_vma=False,
    )
```

profile of v0, /device:TPU:0, one launch (start us, length us, event | category | flops | bytes accessed | tf_op | source)
XLA Modules:
  0.0 222.3 jit_solution(6501743802325076783)
XLA Ops:
  8.8 0.7 broadcast_select_fusion.1
  9.9 1.0 and_and_fusion.1
  10.9 47.4 %all-gather.2.cloned.1.call-done = bf16[512,2048]{1,0:T(8,128)(2,1)} async-done(((bf16[512,512]{1,0:T(8,128)(2,1)}), bf16[512,2048]{1,0:T(8,128)(2,1)}) %all-gather.2.cloned.1.call-update) | async-done | bytes 2097168 | tf_op jit(solution)/shard_map/all_gather | solution.py:48
  58.3 2.2 %fusion.17 = f32[512]{0:T(512)S(1)} fusion(bf16[512,2048]{1,0:T(8,128)(2,1)} %all-gather.2.cloned.1.call-done), kind=kLoop, calls=%fused_computation.26 | loop fusion | flops 3145216 | bytes 2099200 | tf_op jit(solution)/shard_map/reduce_sum | solution.py:50
  60.5 2.8 %fusion.49 = f32[512,256]{0,1:T(8,128)S(1)} fusion(bf16[2048,256]{1,0:T(8,128)(2,1)} %param.14, bf16[512,2048]{1,0:T(8,128)(2,1)} %all-gather.2.cloned.1.call-done, f32[2048]{0:T(1024)} %param.12, f32[512]{0:T(512)S(1)} %add_rsqrt_fusion), kind=kOutput, calls=%fused_computation.84 | convolution fusion | flops 541065216 | bytes 3680256 | tf_op jit(solution)/shard_map/dot_general | solution.py:60
  63.4 0.9 fusion.46
  64.6 0.9 convolution_convert_fusion.1
  65.7 0.9 select_reduce_fusion.1
  66.6 0.9 fusion.21
  67.6 1.9 fusion.28
  69.8 2.9 %scatter_custom_fusion.1 = bf16[1024,512]{1,0:T(8,128)(2,1)S(1)} fusion(s32[512]{0:T(512)S(1)} %bitcast.76, bf16[512,512]{1,0:T(8,128)(2,1)S(1)} %copy.24, bf16[]{:T(256)} %constant.109.clone.1), kind=kCustom, calls=%fused_computation.44 | custom fusion | bytes 1048578 | tf_op jit(solution)/shard_map/scatter | solution.py:116
  72.7 88.9 %while.27 = (s32[]{:T(128)}, bf16[512,512]{0,1:T(8,128)(2,1)S(1)}, s32[512]{0:T(512)S(1)}, s32[512]{0:T(512)S(1)}, f32[4,512]{1,0:T(4,128)S(1)}, /*index=5*/f32[...) while((s32[]{:T(128)}, bf16[512,512]{0,1:T(8,128)(2,1)S(1)}, ...), condition=%wide.region_8.9_spmd.clone.clone, body=%wide.region_4.8_spmd.clone.clone.sunk | while | flops 281293824 | bytes 21409060 | solution.py:136
  72.7 1.7 collective-permute-start.2
  74.4 3.7 %collective-permute-start.1 = (s32[512]{0:T(512)S(1)}, s32[512]{0:T(512)S(1)}, u32[]{:S(2)}, u32[]{:S(2)}) collective-permute-start(s32[512]{0:T(512)S(1)} %get-tuple-element.427), channel_id=1, source_target_pairs={{0,4},{4,8},{8,12},{12,16},{16,20},{20,24},{24,28},{1,5},{5,9},{9,... | collective-permute-start | bytes 6152 | tf_op jit(solution)/shard_map/while/body/eval_jaxpr/ppermute | solution.py:18
  78.1 2.0 collective-permute-start
  80.5 1.1 collective-permute-done
  81.6 0.9 select_reduce_fusion.3
  82.5 0.9 fusion.65
  83.4 2.9 %fusion.66 = f32[512,4,64]{0,2,1:T(8,128)} fusion(f32[4,512,512]{1,2,0:T(8,128)S(1)} %get-tuple-element.408, f32[4,512]{1,0:T(4,128)S(1)} %get-tuple-element.443, pred[512,512]{0,1:T(8,128)(4,1)S(1)} %and_and_fusion.3, f32[512,4,64]{0,2,1:T(8,128)} %get-tuple-element.431, bf16[512,4,2,64]{0,3,2,1:T(8,128)(2,1)S(1)} %bitcast.69, ...), kind=kOutput, calls=%fused_computation.10.clone.1 | convolution fusion | flops 138674176 | bytes 5783552 | tf_op jit(solution)/shard_map/while/body/eval_jaxpr/hqk,khd->qhd/dot_general | solution.py:95
  86.6 3.0 %scatter_fusion = bf16[1024,512]{1,0:T(8,128)(2,1)S(1)} fusion(bf16[1024,512]{1,0:T(8,128)(2,1)S(1)} %get-tuple-element.432, s32[512]{0:T(512)S(1)} %get-tuple-element.410, bf16[512,512]{1,0:T(8,128)(2,1)S(1)} %copy.30), kind=kCustom, calls=%fused_computation.clone.clone.clone.1 | custom fusion | bytes 1574912 | tf_op jit(solution)/shard_map/while/body/eval_jaxpr/scatter | solution.py:116
  89.6 8.1 %collective-permute-start.2 = (s32[512]{0:T(512)S(1)}, s32[512]{0:T(512)S(1)}, u32[]{:S(2)}, u32[]{:S(2)}) collective-permute-start(s32[512]{0:T(512)S(1)} %get-tuple-element.428), channel_id=1, source_target_pairs={{0,4},{4,8},{8,12},{12,16},{16,20},{20,24},{24,28},{1,5},{5,9},{9,... | collective-permute-start | bytes 6152 | tf_op jit(solution)/shard_map/while/body/eval_jaxpr/ppermute | solution.py:18
  97.7 4.4 %collective-permute-start.1 = (s32[512]{0:T(512)S(1)}, s32[512]{0:T(512)S(1)}, u32[]{:S(2)}, u32[]{:S(2)}) collective-permute-start(s32[512]{0:T(512)S(1)} %get-tuple-element.427), channel_id=1, source_target_pairs={{0,4},{4,8},{8,12},{12,16},{16,20},{20,24},{24,28},{1,5},{5,9},{9,... | collective-permute-start | bytes 6152 | tf_op jit(solution)/shard_map/while/body/eval_jaxpr/ppermute | solution.py:18
  102.1 2.0 collective-permute-start
  104.4 1.1 collective-permute-done
  105.5 0.9 select_reduce_fusion.3
  106.4 0.9 fusion.65
  107.4 2.9 %fusion.66 = f32[512,4,64]{0,2,1:T(8,128)} fusion(f32[4,512,512]{1,2,0:T(8,128)S(1)} %get-tuple-element.408, f32[4,512]{1,0:T(4,128)S(1)} %get-tuple-element.443, pred[512,512]{0,1:T(8,128)(4,1)S(1)} %and_and_fusion.3, f32[512,4,64]{0,2,1:T(8,128)} %get-tuple-element.431, bf16[512,4,2,64]{0,3,2,1:T(8,128)(2,1)S(1)} %bitcast.69, ...), kind=kOutput, calls=%fused_computation.10.clone.1 | convolution fusion | flops 138674176 | bytes 5783552 | tf_op jit(solution)/shard_map/while/body/eval_jaxpr/hqk,khd->qhd/dot_general | solution.py:95
  110.5 3.0 %scatter_fusion = bf16[1024,512]{1,0:T(8,128)(2,1)S(1)} fusion(bf16[1024,512]{1,0:T(8,128)(2,1)S(1)} %get-tuple-element.432, s32[512]{0:T(512)S(1)} %get-tuple-element.410, bf16[512,512]{1,0:T(8,128)(2,1)S(1)} %copy.30), kind=kCustom, calls=%fused_computation.clone.clone.clone.1 | custom fusion | bytes 1574912 | tf_op jit(solution)/shard_map/while/body/eval_jaxpr/scatter | solution.py:116
  113.5 8.9 %collective-permute-start.2 = (s32[512]{0:T(512)S(1)}, s32[512]{0:T(512)S(1)}, u32[]{:S(2)}, u32[]{:S(2)}) collective-permute-start(s32[512]{0:T(512)S(1)} %get-tuple-element.428), channel_id=1, source_target_pairs={{0,4},{4,8},{8,12},{12,16},{16,20},{20,24},{24,28},{1,5},{5,9},{9,... | collective-permute-start | bytes 6152 | tf_op jit(solution)/shard_map/while/body/eval_jaxpr/ppermute | solution.py:18
  122.5 4.4 %collective-permute-start.1 = (s32[512]{0:T(512)S(1)}, s32[512]{0:T(512)S(1)}, u32[]{:S(2)}, u32[]{:S(2)}) collective-permute-start(s32[512]{0:T(512)S(1)} %get-tuple-element.427), channel_id=1, source_target_pairs={{0,4},{4,8},{8,12},{12,16},{16,20},{20,24},{24,28},{1,5},{5,9},{9,... | collective-permute-start | bytes 6152 | tf_op jit(solution)/shard_map/while/body/eval_jaxpr/ppermute | solution.py:18
  126.9 2.0 collective-permute-start
  129.2 1.1 collective-permute-done
  130.3 0.9 select_reduce_fusion.3
  131.3 0.9 fusion.65
  132.2 2.9 %fusion.66 = f32[512,4,64]{0,2,1:T(8,128)} fusion(f32[4,512,512]{1,2,0:T(8,128)S(1)} %get-tuple-element.408, f32[4,512]{1,0:T(4,128)S(1)} %get-tuple-element.443, pred[512,512]{0,1:T(8,128)(4,1)S(1)} %and_and_fusion.3, f32[512,4,64]{0,2,1:T(8,128)} %get-tuple-element.431, bf16[512,4,2,64]{0,3,2,1:T(8,128)(2,1)S(1)} %bitcast.69, ...), kind=kOutput, calls=%fused_computation.10.clone.1 | convolution fusion | flops 138674176 | bytes 5783552 | tf_op jit(solution)/shard_map/while/body/eval_jaxpr/hqk,khd->qhd/dot_general | solution.py:95
  135.3 3.0 %scatter_fusion = bf16[1024,512]{1,0:T(8,128)(2,1)S(1)} fusion(bf16[1024,512]{1,0:T(8,128)(2,1)S(1)} %get-tuple-element.432, s32[512]{0:T(512)S(1)} %get-tuple-element.410, bf16[512,512]{1,0:T(8,128)(2,1)S(1)} %copy.30), kind=kCustom, calls=%fused_computation.clone.clone.clone.1 | custom fusion | bytes 1574912 | tf_op jit(solution)/shard_map/while/body/eval_jaxpr/scatter | solution.py:116
  138.3 7.4 %collective-permute-start.2 = (s32[512]{0:T(512)S(1)}, s32[512]{0:T(512)S(1)}, u32[]{:S(2)}, u32[]{:S(2)}) collective-permute-start(s32[512]{0:T(512)S(1)} %get-tuple-element.428), channel_id=1, source_target_pairs={{0,4},{4,8},{8,12},{12,16},{16,20},{20,24},{24,28},{1,5},{5,9},{9,... | collective-permute-start | bytes 6152 | tf_op jit(solution)/shard_map/while/body/eval_jaxpr/ppermute | solution.py:18
  145.8 4.4 %collective-permute-start.1 = (s32[512]{0:T(512)S(1)}, s32[512]{0:T(512)S(1)}, u32[]{:S(2)}, u32[]{:S(2)}) collective-permute-start(s32[512]{0:T(512)S(1)} %get-tuple-element.427), channel_id=1, source_target_pairs={{0,4},{4,8},{8,12},{12,16},{16,20},{20,24},{24,28},{1,5},{5,9},{9,... | collective-permute-start | bytes 6152 | tf_op jit(solution)/shard_map/while/body/eval_jaxpr/ppermute | solution.py:18
  150.2 2.0 collective-permute-start
  152.5 1.1 collective-permute-done
  153.6 0.9 select_reduce_fusion.3
  154.5 0.9 fusion.65
  155.5 2.9 %fusion.66 = f32[512,4,64]{0,2,1:T(8,128)} fusion(f32[4,512,512]{1,2,0:T(8,128)S(1)} %get-tuple-element.408, f32[4,512]{1,0:T(4,128)S(1)} %get-tuple-element.443, pred[512,512]{0,1:T(8,128)(4,1)S(1)} %and_and_fusion.3, f32[512,4,64]{0,2,1:T(8,128)} %get-tuple-element.431, bf16[512,4,2,64]{0,3,2,1:T(8,128)(2,1)S(1)} %bitcast.69, ...), kind=kOutput, calls=%fused_computation.10.clone.1 | convolution fusion | flops 138674176 | bytes 5783552 | tf_op jit(solution)/shard_map/while/body/eval_jaxpr/hqk,khd->qhd/dot_general | solution.py:95
  158.6 3.0 %scatter_fusion = bf16[1024,512]{1,0:T(8,128)(2,1)S(1)} fusion(bf16[1024,512]{1,0:T(8,128)(2,1)S(1)} %get-tuple-element.432, s32[512]{0:T(512)S(1)} %get-tuple-element.410, bf16[512,512]{1,0:T(8,128)(2,1)S(1)} %copy.30), kind=kCustom, calls=%fused_computation.clone.clone.clone.1 | custom fusion | bytes 1574912 | tf_op jit(solution)/shard_map/while/body/eval_jaxpr/scatter | solution.py:116
  161.6 1.5 divide_convert_fusion
  163.1 2.1 convolution_convert_fusion
  165.2 48.2 %reduce-scatter.2.cloned.1.call-done = bf16[512,512]{1,0:T(8,128)(2,1)} async-done(((bf16[512,2048]{1,0:T(8,128)(2,1)}), bf16[512,512]{1,0:T(8,128)(2,1)}) %reduce-scatter.2.cloned.1.call-update) | async-done | bytes 524304 | tf_op jit(solution)/shard_map/reduce_scatter | solution.py:144
  213.5 2.0 add_convert_fusion
  (88 shorter events, 5.2 us)
Async XLA Ops:
  7.2 156.0 %copy-start = (bf16[256,2048]{1,0:T(8,128)(2,1)S(1)}, bf16[256,2048]{1,0:T(8,128)(2,1)}, u32[]{:S(2)}) copy-start(bf16[256,2048]{1,0:T(8,128)(2,1)} %param.16) | copy-start | bytes 3145732
  7.2 56.2 %copy-start.7 = (f32[2048]{0:T(1024)S(1)}, f32[2048]{0:T(1024)}, u32[]{:S(2)}) copy-start(f32[2048]{0:T(1024)} %param.12) | copy-start | bytes 24580
  7.2 56.1 %copy-start.5 = (bf16[2048,256]{1,0:T(8,128)(2,1)S(1)}, bf16[2048,256]{1,0:T(8,128)(2,1)}, u32[]{:S(2)}) copy-start(bf16[2048,256]{1,0:T(8,128)(2,1)} %param.13) | copy-start | bytes 3145732
  7.2 51.1 %all-gather.2.cloned.1.call-start = ((), (), s32[]{:S(2)}) async-start(), calls=%async_computation.1 | async-start | bytes 2621440 | tf_op jit(solution)/shard_map/all_gather | solution.py:48
  7.9 205.5 %reduce-scatter.2.cloned.1.call-start = ((), (), s32[]{:S(2)}) async-start(), calls=%async_computation.2 | async-start | bytes 2621440 | tf_op jit(solution)/shard_map/reduce_scatter | solution.py:144
  58.3 5.1 %copy-start.3 = (bf16[512,2048]{1,0:T(8,128)(2,1)S(1)}, bf16[512,2048]{1,0:T(8,128)(2,1)}, u32[]{:S(2)}) copy-start(bf16[512,2048]{1,0:T(8,128)(2,1)} %all-gather.2.cloned.1.call-done) | copy-start | bytes 6291460
  63.4 1.2 copy-start.6
  67.6 5.1 %copy-start.4 = (s32[512]{0:T(512)S(1)}, s32[512]{0:T(512)}, u32[]{:S(2)}) copy-start(s32[512]{0:T(512)} %param.17) | copy-start | bytes 6148
  72.7 7.4 %collective-permute-start.2 = (s32[512]{0:T(512)S(1)}, s32[512]{0:T(512)S(1)}, u32[]{:S(2)}, u32[]{:S(2)}) collective-permute-start(s32[512]{0:T(512)S(1)} %get-tuple-element.428), channel_id=1, source_target_pairs={{0,4},{4,8},{8,12},{12,16},{16,20},{20,24},{24,28},{1,5},{5,9},{9,... | collective-permute-start | bytes 6152 | tf_op jit(solution)/shard_map/while/body/eval_jaxpr/ppermute | solution.py:18
  74.4 5.7 %collective-permute-start.1 = (s32[512]{0:T(512)S(1)}, s32[512]{0:T(512)S(1)}, u32[]{:S(2)}, u32[]{:S(2)}) collective-permute-start(s32[512]{0:T(512)S(1)} %get-tuple-element.427), channel_id=1, source_target_pairs={{0,4},{4,8},{8,12},{12,16},{16,20},{20,24},{24,28},{1,5},{5,9},{9,... | collective-permute-start | bytes 6152 | tf_op jit(solution)/shard_map/while/body/eval_jaxpr/ppermute | solution.py:18
  78.1 3.4 %collective-permute-start = (bf16[512,512]{0,1:T(8,128)(2,1)S(1)}, bf16[512,512]{0,1:T(8,128)(2,1)S(1)}, u32[]{:S(2)}, u32[]{:S(2)}) collective-permute-start(bf16[512,512]{0,1:T(8,128)(2,1)S(1)} %get-tuple-element.426), channel_id=1, source_target_pairs={{0,4},{4,8},{8,12},{12,16},{16,20},{20,24},{24,28},{1,5},{5,9},{9,... | collective-permute-start | bytes 1572872 | tf_op jit(solution)/shard_map/while/body/eval_jaxpr/ppermute | solution.py:18
  89.6 14.5 %collective-permute-start.2 = (s32[512]{0:T(512)S(1)}, s32[512]{0:T(512)S(1)}, u32[]{:S(2)}, u32[]{:S(2)}) collective-permute-start(s32[512]{0:T(512)S(1)} %get-tuple-element.428), channel_id=1, source_target_pairs={{0,4},{4,8},{8,12},{12,16},{16,20},{20,24},{24,28},{1,5},{5,9},{9,... | collective-permute-start | bytes 6152 | tf_op jit(solution)/shard_map/while/body/eval_jaxpr/ppermute | solution.py:18
  97.7 6.4 %collective-permute-start.1 = (s32[512]{0:T(512)S(1)}, s32[512]{0:T(512)S(1)}, u32[]{:S(2)}, u32[]{:S(2)}) collective-permute-start(s32[512]{0:T(512)S(1)} %get-tuple-element.427), channel_id=1, source_target_pairs={{0,4},{4,8},{8,12},{12,16},{16,20},{20,24},{24,28},{1,5},{5,9},{9,... | collective-permute-start | bytes 6152 | tf_op jit(solution)/shard_map/while/body/eval_jaxpr/ppermute | solution.py:18
  102.1 3.4 %collective-permute-start = (bf16[512,512]{0,1:T(8,128)(2,1)S(1)}, bf16[512,512]{0,1:T(8,128)(2,1)S(1)}, u32[]{:S(2)}, u32[]{:S(2)}) collective-permute-start(bf16[512,512]{0,1:T(8,128)(2,1)S(1)} %get-tuple-element.426), channel_id=1, source_target_pairs={{0,4},{4,8},{8,12},{12,16},{16,20},{20,24},{24,28},{1,5},{5,9},{9,... | collective-permute-start | bytes 1572872 | tf_op jit(solution)/shard_map/while/body/eval_jaxpr/ppermute | solution.py:18
  113.5 15.4 %collective-permute-start.2 = (s32[512]{0:T(512)S(1)}, s32[512]{0:T(512)S(1)}, u32[]{:S(2)}, u32[]{:S(2)}) collective-permute-start(s32[512]{0:T(512)S(1)} %get-tuple-element.428), channel_id=1, source_target_pairs={{0,4},{4,8},{8,12},{12,16},{16,20},{20,24},{24,28},{1,5},{5,9},{9,... | collective-permute-start | bytes 6152 | tf_op jit(solution)/shard_map/while/body/eval_jaxpr/ppermute | solution.py:18
  122.5 6.4 %collective-permute-start.1 = (s32[512]{0:T(512)S(1)}, s32[512]{0:T(512)S(1)}, u32[]{:S(2)}, u32[]{:S(2)}) collective-permute-start(s32[512]{0:T(512)S(1)} %get-tuple-element.427), channel_id=1, source_target_pairs={{0,4},{4,8},{8,12},{12,16},{16,20},{20,24},{24,28},{1,5},{5,9},{9,... | collective-permute-start | bytes 6152 | tf_op jit(solution)/shard_map/while/body/eval_jaxpr/ppermute | solution.py:18
  126.9 3.4 %collective-permute-start = (bf16[512,512]{0,1:T(8,128)(2,1)S(1)}, bf16[512,512]{0,1:T(8,128)(2,1)S(1)}, u32[]{:S(2)}, u32[]{:S(2)}) collective-permute-start(bf16[512,512]{0,1:T(8,128)(2,1)S(1)} %get-tuple-element.426), channel_id=1, source_target_pairs={{0,4},{4,8},{8,12},{12,16},{16,20},{20,24},{24,28},{1,5},{5,9},{9,... | collective-permute-start | bytes 1572872 | tf_op jit(solution)/shard_map/while/body/eval_jaxpr/ppermute | solution.py:18
  138.3 13.8 %collective-permute-start.2 = (s32[512]{0:T(512)S(1)}, s32[512]{0:T(512)S(1)}, u32[]{:S(2)}, u32[]{:S(2)}) collective-permute-start(s32[512]{0:T(512)S(1)} %get-tuple-element.428), channel_id=1, source_target_pairs={{0,4},{4,8},{8,12},{12,16},{16,20},{20,24},{24,28},{1,5},{5,9},{9,... | collective-permute-start | bytes 6152 | tf_op jit(solution)/shard_map/while/body/eval_jaxpr/ppermute | solution.py:18
  145.8 6.4 %collective-permute-start.1 = (s32[512]{0:T(512)S(1)}, s32[512]{0:T(512)S(1)}, u32[]{:S(2)}, u32[]{:S(2)}) collective-permute-start(s32[512]{0:T(512)S(1)} %get-tuple-element.427), channel_id=1, source_target_pairs={{0,4},{4,8},{8,12},{12,16},{16,20},{20,24},{24,28},{1,5},{5,9},{9,... | collective-permute-start | bytes 6152 | tf_op jit(solution)/shard_map/while/body/eval_jaxpr/ppermute | solution.py:18
  150.2 3.4 %collective-permute-start = (bf16[512,512]{0,1:T(8,128)(2,1)S(1)}, bf16[512,512]{0,1:T(8,128)(2,1)S(1)}, u32[]{:S(2)}, u32[]{:S(2)}) collective-permute-start(bf16[512,512]{0,1:T(8,128)(2,1)S(1)} %get-tuple-element.426), channel_id=1, source_target_pairs={{0,4},{4,8},{8,12},{12,16},{16,20},{20,24},{24,28},{1,5},{5,9},{9,... | collective-permute-start | bytes 1572872 | tf_op jit(solution)/shard_map/while/body/eval_jaxpr/ppermute | solution.py:18
  161.6 53.8 %copy-start.1 = (bf16[1024,512]{1,0:T(8,128)(2,1)}, bf16[1024,512]{1,0:T(8,128)(2,1)S(1)}, u32[]{:S(2)}) copy-start(bf16[1024,512]{1,0:T(8,128)(2,1)S(1)} %get-tuple-element.220) | copy-start | bytes 3145732
  161.6 51.8 %copy-start.2 = (bf16[512,512]{1,0:T(8,128)(2,1)S(1)}, bf16[512,512]{1,0:T(8,128)(2,1)}, u32[]{:S(2)}) copy-start(bf16[512,512]{1,0:T(8,128)(2,1)} %param.11) | copy-start | bytes 1572868
Sparse Core Ops, SparseCore 0:
  9.6 48.6 all-gather.1
  165.4 48.0 reduce-scatter.1
where the time goes:
time: 223 us; the launch traced here: 222 us
  waiting for transfers between devices  101 us (45%)
  starting transfers between devices  50.9 us (23%)
  matrix products  24.8 us (11%)
  local copies, waits for them, and re-layouts  16.2 us (7%)
  other arithmetic  14.9 us (7%)
  between operations  14.3 us (6%)
    ppermute x12, starting transfers between devices, passed_along(): return lax.ppermute(x, axis, pairs)  50.8 us
    reduce_scatter x1, waiting for transfers between devices, body(): lax.psum_scatter(projected.astype(jnp.bfloat16), 'tp', scatter_dimension=...  48.2 us
    all_gather x1, waiting for transfers between devices, body(): gathered = lax.all_gather(residual, 'tp', axis=1, tiled=True)  47.4 us
    scatter x5, local copies, waits for them, and re-layouts, absorb(): cache_rows = cache_rows.at[target].set(incoming[0], mode='drop')  14.7 us
    dot_general x5, matrix products, attend_block(): jnp.einsum('hqk,khd->qhd', weights.astype(jnp.bfloat16), key_value[:, :,...  13.5 us
    reduce_sum x5, other arithmetic, attend_block(): norm_sum = norm_sum * shrink + jnp.sum(weights, axis=2)  4.57 us
    dot_general x5, matrix products, attend_block(): jnp.einsum('qhd,khd->hqk', queries, key_value[:, :, 0, :], preferred_elem...  4.54 us
  transfers between devices with their start and end apart: 14, of which 6 were waited for; matrix products, arithmetic and copies ran while one was open for 2% of the time, Pallas kernels for 0%

commit v1 on v0

v1 whole, which is shorter than its diff:
```python
import functools

import jax
import jax.numpy as jnp
from jax import lax
from jax.experimental import pallas as pl
from jax.experimental.pallas import tpu as pltpu
from jax.sharding import PartitionSpec as P

HD = 64
PAGE = 128
SPAN = 16
THETA = 130000.0
EPS = 1e-05
MESH = pl.DeviceIdType.MESH
F32 = jnp.float32
BF16 = jnp.bfloat16


def kernel(
    S, T, R, G,
    res_ref, gain_ref, wq_ref, wk_ref, wv_ref, wo_ref, cos_ref, sin_ref, seg_ref, valid_ref, meta_ref,
    hid_ref, cache_ref,
    gath, nbuf, qpad, kv, meta, att, wo_all, bias,
    z_recv, zl_send, zr_send, wo_send, wo_recv, bc_send, bc_recv, meta_send, meta_recv,
    kv_send, kv_recv, sib_send, att_send, att_recv,
):
    i = lax.axis_index("seq")
    t = lax.axis_index("tp")
    rows_all, width = res_ref.shape
    C = rows_all // PAGE
    HL = wq_ref.shape[1] // HD
    core = lax.rem(i, 2)
    sib = i + 1 - 2 * core
    g = lax.rem(i, G)
    base = i - g
    wrows = wo_ref.shape[0] // G

    far = max(R, G - 1)
    barrier = pltpu.get_barrier_semaphore()
    for d in range(1, far + 1):
        @pl.when(i + d < S)
        def _(d=d):
            pl.semaphore_signal(barrier, inc=1, device_id=(i + d, t), device_id_type=MESH)

        @pl.when(i - d >= 0)
        def _(d=d):
            pl.semaphore_signal(barrier, inc=1, device_id=(i - d, t), device_id_type=MESH)
    for k in range(1, T):
        pl.semaphore_signal(barrier, inc=1, device_id=(i, lax.rem(t + k, T)), device_id_type=MESH)
    pl.semaphore_wait(barrier, jnp.minimum(i, far) + jnp.minimum(S - 1 - i, far) + (T - 1))

    def rows_of(c):
        return pl.ds(pl.multiple_of(c * PAGE, PAGE), PAGE)

    def wo_copy(s, to):
        r = pl.ds(pl.multiple_of(g * wrows, wrows), wrows)
        return pltpu.make_async_remote_copy(
            src_ref=wo_ref.at[r, pl.ds(pl.multiple_of(to * width, width), width)],
            dst_ref=wo_all.at[s, r, :],
            send_sem=wo_send.at[to], recv_sem=wo_recv.at[s],
            device_id=(i, to), device_id_type=MESH)

    def bc_copy(owner, to):
        r = pl.ds(pl.multiple_of(owner * wrows, wrows), wrows)
        return pltpu.make_async_remote_copy(
            src_ref=wo_all.at[:, r, :], dst_ref=wo_all.at[:, r, :],
            send_sem=bc_send.at[to], recv_sem=bc_recv.at[owner],
            device_id=(base + to, t), device_id_type=MESH)

    def meta_copy(d):
        return pltpu.make_async_remote_copy(
            src_ref=meta_ref, dst_ref=meta.at[d - 1],
            send_sem=meta_send.at[d - 1], recv_sem=meta_recv.at[d - 1],
            device_id=(i + d, t), device_id_type=MESH)

    def z_copy(s, c, step, own):
        r = rows_of(c)
        sems = zr_send if step > 0 else zl_send
        return pltpu.make_async_remote_copy(
            src_ref=res_ref.at[r, :] if own else gath.at[s, r, :],
            dst_ref=gath.at[s, r, :],
            send_sem=sems.at[s, c], recv_sem=z_recv.at[s, c],
            device_id=(i, t + step), device_id_type=MESH)

    def kv_copy(d, c):
        r = rows_of(c)
        return pltpu.make_async_remote_copy(
            src_ref=kv.at[0, r, :], dst_ref=kv.at[d, r, :],
            send_sem=kv_send.at[d, c], recv_sem=kv_recv.at[d, c],
            device_id=(i + d, t), device_id_type=MESH)

    def sib_copy(src, dst, c):
        r = rows_of(c)
        return pltpu.make_async_remote_copy(
            src_ref=kv.at[src, r, :], dst_ref=kv.at[dst, r, :],
            send_sem=sib_send.at[dst, c], recv_sem=kv_recv.at[dst, c],
            device_id=(sib, t), device_id_type=MESH)

    def att_copy(s, to, c):
        r = rows_of(c)
        return pltpu.make_async_remote_copy(
            src_ref=att.at[s, r, :], dst_ref=att.at[s, r, :],
            send_sem=att_send.at[to, c], recv_sem=att_recv.at[s, c],
            device_id=(i, to), device_id_type=MESH)

    def send_own(c):
        @pl.when(t + 1 < T)
        def _():
            z_copy(t, c, 1, True).start()

        @pl.when(t >= 1)
        def _():
            z_copy(t, c, -1, True).start()

    send_own(0)
    for k in range(1, T):
        wo_copy(t, lax.rem(t + k, T)).start()
    if C > 1:
        send_own(1)
    for d in range(1, R + 1):
        @pl.when(i + d < S)
        def _(d=d):
            meta_copy(d).start()

    gath[t] = res_ref[...]
    mine = pl.ds(pl.multiple_of(g * wrows, wrows), wrows)
    wo_all[t, mine, :] = wo_ref[mine, pl.ds(pl.multiple_of(t * width, width), width)]
    for d in range(1, R + 1):
        @pl.when(i < d)
        def _(d=d):
            kv[d] = jnp.zeros(kv.shape[1:], BF16)
            meta[d - 1] = jnp.full(meta.shape[1:], -1, jnp.int32)

    lane128 = lax.broadcasted_iota(jnp.int32, (PAGE, 128), 1)
    low = lane128 < HD
    first = lax.rem(lane128, HD) < HD // 2

    def rotated(x, cs, sn):
        fwd = pltpu.roll(x, 128 - HD // 2, 1)
        back = pltpu.roll(x, HD // 2, 1)
        return x * cs + jnp.where(first, fwd, back) * sn

    def forward_kv(c):
        for m in range(1, R // 2 + 1):
            d = 2 * m

            @pl.when(i - d >= 0)
            def _(d=d):
                kv_copy(d, c).wait_recv()

                @pl.when(core == 1)
                def _():
                    sib_copy(d, d - 1, c).start()

                if d + 1 <= R:
                    @pl.when(core == 0)
                    def _():
                        sib_copy(d, d + 1, c).start()

    def gather_step(c, carry):
        for k in range(1, T):
            @pl.when(t - k >= 0)
            def _(k=k):
                z_copy(t - k, c, 1, False).wait_recv()

                @pl.when(t + 1 < T)
                def _():
                    z_copy(t - k, c, 1, False).start()

            @pl.when(t + k < T)
            def _(k=k):
                z_copy(t + k, c, -1, False).wait_recv()

                @pl.when(t >= 1)
                def _():
                    z_copy(t + k, c, -1, False).start()

        @pl.when(c + 2 < C)
        def _():
            send_own(c + 2)

        r = rows_of(c)
        total = jnp.zeros((PAGE, 1), F32)
        for s in range(T):
            x = gath[s, r, :].astype(F32)
            total = total + jnp.sum(x * x, axis=1, keepdims=True)
        scale = lax.rsqrt(total / (T * width) + EPS)
        for s in range(T):
            cols = slice(s * width, (s + 1) * width)
            x = gath[s, r, :].astype(F32)
            nbuf[:, cols] = (x * scale * gain_ref[:, cols]).astype(BF16)
        n = nbuf[...]
        k_raw = jnp.dot(n, wk_ref[...], preferred_element_type=F32)
        v_raw = jnp.dot(n, wv_ref[...], preferred_element_type=F32)
        cs = cos_ref[r, :]
        sn = sin_ref[r, :]
        ok = valid_ref[r, :]
        for pair in range(HL // 2):
            cols = slice(pair * 128, (pair + 1) * 128)
            kr = rotated(k_raw[:, cols], cs, sn) * ok
            vr = v_raw[:, cols] * ok
            kv[0, r, pair * 256:pair * 256 + 128] = jnp.where(low, kr, pltpu.roll(vr, HD, 1)).astype(BF16)
            kv[0, r, pair * 256 + 128:pair * 256 + 256] = jnp.where(low, pltpu.roll(kr, HD, 1), vr).astype(BF16)
        for m in range(1, R // 2 + 1):
            @pl.when(i + 2 * m < S)
            def _(m=m):
                kv_copy(2 * m, c).start()

        @pl.when(core == 0)
        def _():
            sib_copy(0, 1, c).start()

        q_raw = jnp.dot(n, wq_ref[...], preferred_element_type=F32)
        for pair in range(HL // 2):
            cols = slice(pair * 128, (pair + 1) * 128)
            qr = rotated(q_raw[:, cols], cs, sn) * (HD ** -0.5)
            qpad[r, pair * 256:pair * 256 + 128] = jnp.where(low, qr, 0.0).astype(BF16)
            qpad[r, pair * 256 + 128:pair * 256 + 256] = jnp.where(low, pltpu.roll(qr, HD, 1), 0.0).astype(BF16)

        @pl.when(c == 0)
        def _():
            for k in range(1, T):
                wo_copy(lax.rem(t + k, T), t).wait_recv()
            for k in range(1, G):
                bc_copy(g, lax.rem(g + k, G)).start()

        @pl.when(c >= 1)
        def _():
            forward_kv(c - 1)
        return carry

    lax.fori_loop(0, C, gather_step, 0)
    forward_kv(C - 1)

    for d in range(1, R + 1):
        @pl.when(i >= d)
        def _(d=d):
            meta_copy(d).wait_recv()
            if d % 2 == 1:
                for c in range(C):
                    kv_copy(d, c).wait_recv()
    for k in range(1, G):
        bc_copy(lax.rem(g + k, G), g).wait_recv()

    keys = rows_all
    slot_count = cache_ref.shape[0]

    def attend_step(c, carry):
        @pl.when(c < C)
        def _():
            r = rows_of(c)
            seg = seg_ref[r, :][:, 0:1]
            q_place = c * PAGE + lax.broadcasted_iota(jnp.int32, (PAGE, keys), 0)
            k_place = lax.broadcasted_iota(jnp.int32, (PAGE, keys), 1)
            for d in range(R + 1):
                group = meta_ref[0:1, :] if d == 0 else meta[d - 1, 0:1, :]
                allowed = group == seg
                if d == 0:
                    allowed = allowed & (k_place <= q_place)
                bias[d] = jnp.where(allowed, 0.0, -1e30)
            outs = []
            for h in range(HL):
                cols = slice(h * 128, (h + 1) * 128)
                q = qpad[r, cols]
                scores = []
                top = None
                for d in range(R + 1):
                    s = lax.dot_general(q, kv[d, :, cols], (((1,), (1,)), ((), ())), preferred_element_type=F32) + bias[d]
                    scores.append(s)
                    here = jnp.max(s, axis=1, keepdims=True)
                    top = here if top is None else jnp.maximum(top, here)
                den = None
                acc = None
                for d in range(R + 1):
                    e = jnp.exp(scores[d] - top)
                    part = jnp.sum(e, axis=1, keepdims=True)
                    den = part if den is None else den + part
                    o = jnp.dot(e.astype(BF16), kv[d, :, cols], preferred_element_type=F32)
                    acc = o if acc is None else acc + o
                outs.append(acc / den)
            for pair in range(HL // 2):
                both = jnp.where(low, pltpu.roll(outs[2 * pair], HD, 1), outs[2 * pair + 1])
                att[t, r, pair * 128:(pair + 1) * 128] = both.astype(BF16)
            for k in range(1, T):
                att_copy(t, lax.rem(t + k, T), c).start()
            for j in range(slot_count // C):
                slot = c * (slot_count // C) + j
                page = jnp.zeros((PAGE, kv.shape[2]), BF16)
                for b in range(2):
                    for p in range(C):
                        src = meta_ref[8 + p:9 + p, :] if b == 0 else meta[0, 8 + p:9 + p, :]
                        hit = jnp.where(src == i * slot_count + slot, 1.0, 0.0).astype(BF16)
                        page = page + kv[b, p * PAGE:(p + 1) * PAGE, :] * hit
                cache_ref[slot] = page

        @pl.when(c >= 1)
        def _():
            r = rows_of(c - 1)
            for k in range(1, T):
                att_copy(lax.rem(t + k, T), t, c - 1).wait_recv()
            acc = res_ref[r, :].astype(F32)
            proj = jnp.dot(att[0, r, :], wo_all[0], preferred_element_type=F32)
            for s in range(1, T):
                proj = proj + jnp.dot(att[s, r, :], wo_all[s], preferred_element_type=F32)
            hid_ref[r, :] = (acc + proj).astype(BF16)
        return carry

    lax.fori_loop(0, C + 1, attend_step, 0)

    for k in range(1, T):
        wo_copy(t, lax.rem(t + k, T)).wait_send()
    for k in range(1, G):
        bc_copy(g, lax.rem(g + k, G)).wait_send()
    for d in range(1, R + 1):
        @pl.when(i + d < S)
        def _(d=d):
            meta_copy(d).wait_send()

    def drain(c, carry):
        for s in range(T):
            @pl.when((t + 1 < T) & (s <= t))
            def _(s=s):
                z_copy(s, c, 1, False).wait_send()

            @pl.when((t >= 1) & (s >= t))
            def _(s=s):
                z_copy(s, c, -1, False).wait_send()
        for m in range(1, R // 2 + 1):
            d = 2 * m

            @pl.when(i + d < S)
            def _(d=d):
                kv_copy(d, c).wait_send()

            @pl.when((i - d >= 0) & (core == 1))
            def _(d=d):
                sib_copy(d, d - 1, c).wait_send()

            if d + 1 <= R:
                @pl.when((i - d >= 0) & (core == 0))
                def _(d=d):
                    sib_copy(d, d + 1, c).wait_send()

        @pl.when(core == 0)
        def _():
            sib_copy(0, 1, c).wait_send()
        for k in range(1, T):
            att_copy(t, lax.rem(t + k, T), c).wait_send()
        return carry

    lax.fori_loop(0, C, drain, 0)


def body(
    S, T,
    residual, norm_gain, query_weight, key_weight, value_weight, out_weight, segment_start, token_valid, page_slot,
):
    rows, width = residual.shape
    local_heads = query_weight.shape[1] // HD
    R = min(SPAN, S // 2)
    G = min(8, S)
    C = rows // PAGE
    pages = page_slot.shape[0]
    slot_count = 2 * pages
    kvw = local_heads * 2 * HD
    first_row = lax.axis_index("seq") * rows
    offset = (first_row + jnp.arange(rows, dtype=jnp.int32) - segment_start).astype(F32)
    frequency = THETA ** (-2.0 * jnp.arange(HD // 2, dtype=F32) / HD)
    angles = offset[:, None] * frequency[None, :]
    cosine = jnp.cos(angles)
    sine = jnp.sin(angles)
    cos_t = jnp.concatenate([cosine] * 4, axis=1)
    sin_t = jnp.concatenate([-sine, sine, -sine, sine], axis=1)
    seg_t = jnp.broadcast_to(segment_start[:, None], (rows, 128))
    valid_t = jnp.broadcast_to((token_valid > 0).astype(F32)[:, None], (rows, 128))
    group = jnp.where(token_valid > 0, segment_start, -1)
    meta_t = jnp.concatenate([
        jnp.broadcast_to(group[None, :], (8, rows)),
        jnp.broadcast_to(page_slot[:, None], (pages, rows)),
        jnp.full((8 - pages, rows), -1, jnp.int32),
    ], axis=0)
    dma = pltpu.SemaphoreType.DMA
    vmem = pl.BlockSpec(memory_space=pltpu.VMEM)
    hidden, cache = pl.pallas_call(
        functools.partial(kernel, S, T, R, G),
        out_shape=(
            jax.ShapeDtypeStruct((rows, width), BF16),
            jax.ShapeDtypeStruct((slot_count, PAGE, kvw), BF16),
        ),
        in_specs=[vmem] * 11,
        out_specs=(vmem, vmem),
        scratch_shapes=[
            pltpu.VMEM((T, rows, width), BF16),
            pltpu.VMEM((PAGE, T * width), BF16),
            pltpu.VMEM((rows, kvw), BF16),
            pltpu.VMEM((R + 1, rows, kvw), BF16),
            pltpu.VMEM((R, 16, rows), jnp.int32),
            pltpu.VMEM((T, rows, local_heads * HD), BF16),
            pltpu.VMEM((T, local_heads * HD, width), BF16),
            pltpu.VMEM((R + 1, PAGE, rows), F32),
            dma((T, C)), dma((T, C)), dma((T, C)),
            dma((T,)), dma((T,)), dma((G,)), dma((G,)), dma((R,)), dma((R,)),
            dma((R + 1, C)), dma((R + 1, C)), dma((R + 1, C)), dma((T, C)), dma((T, C)),
        ],
        compiler_params=pltpu.CompilerParams(
            collective_id=0, has_side_effects=True, vmem_limit_bytes=56 * 1024 * 1024
        ),
        cost_estimate=pl.CostEstimate(flops=4 * 10**9, bytes_accessed=8 * 10**6, transcendentals=5 * 10**6),
    )(residual, norm_gain[None, :], query_weight, key_weight, value_weight, out_weight,
      cos_t, sin_t, seg_t, valid_t, meta_t)
    return hidden, cache


def solution(mesh):
    return jax.shard_map(
        functools.partial(body, mesh.shape["seq"], mesh.shape["tp"]),
        mesh=mesh,
        in_specs=(
            P("seq", "tp"),
            P(),
            P(None, "tp"),
            P(None, "tp"),
            P(None, "tp"),
            P("tp", None),
            P("seq"),
            P("seq"),
            P("seq"),
        ),
        out_specs=(P("seq", "tp"), P("seq", None, "tp")),
        check_vma=False,
    )
```

time: 223 us -> 100 us (0.45)
  the two profiles are of different devices: /device:TPU:0 before, /device:TPU:15 now
where the time goes in v1:
time: 100 us
  Pallas kernels  90.4 us (90%)
  local copies, waits for them, and re-layouts  5.99 us (6%)
  other arithmetic  2.95 us (3%)
    pallas_call x1, Pallas kernels, body(): pl.pallas_call(functools.partial(kernel, S, T, R, G), out_shape=(jax.Shap...  90.4 us
    unnamed x10, local copies, waits for them, and re-layouts  4.19 us

profile of v1, /device:TPU:15, one launch (start us, length us, event | category | flops | bytes accessed | tf_op | source)
XLA Modules:
  0.0 100.1 jit_solution(13468207171821750433)
XLA Ops:
  0.6 0.0 copy-start.3
  0.6 0.6 copy-done.3
  1.3 0.1 pad.1.clone
  1.4 0.0 copy-start.2
  1.4 0.0 copy-start.1
  1.4 0.1 pad.2.clone
  1.5 0.6 copy-done.2
  2.0 0.0 copy-done.1
  2.1 0.7 add_add_fusion.meta_ref
  2.8 0.8 broadcast_in_dim.18.valid_ref
  3.6 0.8 broadcast_in_dim.17.seg_ref
  4.4 1.0 fusion
  5.4 1.3 %pad_maximum_fusion = (f32[512,128]{1,0:T(8,128)}, f32[512,128]{1,0:T(8,128)}) fusion(f32[512,32]{1,0:T(8,128)S(1)} %get-tuple-element.6, f32[512,32]{1,0:T(8,128)S(1)} %get-tuple-element.5, f32[512,32]{1,0:T(8,128)S(1)} %get-tuple-element.4), kind=kLoop, calls=%fused_computation.2 | loop fusion | flops 393216 | bytes 720896 | tf_op jit(solution)/shard_map/concatenate | solution.py:373
  6.7 90.4 %shard_map.104 = (bf16[512,512]{1,0:T(8,128)(2,1)}, bf16[8,128,512]{2,1,0:T(8,128)(2,1)}) custom-call(bf16[512,512]{1,0:T(8,128)(2,1)} %res_ref.1, f32[1,2048]{1,0:T(1,128)} %bitcast.1, bf16[2048,256]{1,0:T(8,128)(2,1)} %wq_ref.1, bf16[2048,256]{1,0:T(8,128)(2,1)} %wk_ref.1, bf16[2048,256]{1,0:T(8,128)(2,1)} %wv_ref.1, bf16[256,2048]{1,0:T(8,128)(2,1)} %wo_ref.1, ...), custom_call_target="tpu_custom_call" | custom-call | flops 4000000000 | bytes 8000000 | tf_op jit(solution)/shard_map/pallas_call | solution.py:385
  97.1 0.0 copy-start
  97.1 2.0 %copy.14 = bf16[512,512]{1,0:T(8,128)(2,1)} copy(bf16[512,512]{1,0:T(8,128)(2,1)} %get-tuple-element.12) | data formatting | bytes 1048576
  99.1 0.0 copy-done
  99.1 1.0 copy.15
  (5 shorter events, 0.0 us)
Async XLA Ops:
  0.6 0.7 copy-start.3
  1.4 0.7 copy-start.2
  1.4 0.7 copy-start.1
  97.1 2.0 %copy-start = (bf16[8,128,512]{2,1,0:T(8,128)(2,1)S(1)}, bf16[8,128,512]{2,1,0:T(8,128)(2,1)}, u32[]{:S(2)}) copy-start(bf16[8,128,512]{2,1,0:T(8,128)(2,1)} %get-tuple-element.13) | copy-start | bytes 3145732

commit v2 on v1

--- a/solution.py
+++ b/solution.py
@@ -19,9 +19,9 @@
 
 def kernel(
     S, T, R, G,
-    res_ref, gain_ref, wq_ref, wk_ref, wv_ref, wo_ref, cos_ref, sin_ref, seg_ref, valid_ref, meta_ref,
+    res_ref, gain_ref, freq_ref, wq_hbm, wk_hbm, wv_hbm, wo_ref, meta_ref,
     hid_ref, cache_ref,
-    gath, nbuf, qpad, kv, meta, att, wo_all, bias,
+    gath, nbuf, qpad, kv, meta, att, wo_all, seg_s, top_s, den_s, acc_s, wq_ref, wk_ref, wv_ref, w_sem,
     z_recv, zl_send, zr_send, wo_send, wo_recv, bc_send, bc_recv, meta_send, meta_recv,
     kv_send, kv_recv, sib_send, att_send, att_recv,
 ):
@@ -36,6 +36,13 @@
     base = i - g
     wrows = wo_ref.shape[0] // G
 
+    loads = [
+        pltpu.make_async_copy(a, b, w_sem.at[n])
+        for n, (a, b) in enumerate(((wk_hbm, wk_ref), (wv_hbm, wv_ref), (wq_hbm, wq_ref)))
+    ]
+    for load in loads:
+        load.start()
+
     far = max(R, G - 1)
     barrier = pltpu.get_barrier_semaphore()
     for d in range(1, far + 1):
@@ -53,6 +60,11 @@
     def rows_of(c):
         return pl.ds(pl.multiple_of(c * PAGE, PAGE), PAGE)
 
+    Q = rows_all // 2
+
+    def half_of(a):
+        return pl.ds(pl.multiple_of(a * Q, Q), Q)
+
     def wo_copy(s, to):
         r = pl.ds(pl.multiple_of(g * wrows, wrows), wrows)
         return pltpu.make_async_remote_copy(
@@ -98,7 +110,7 @@
             device_id=(sib, t), device_id_type=MESH)
 
     def att_copy(s, to, c):
-        r = rows_of(c)
+        r = half_of(c)
         return pltpu.make_async_remote_copy(
             src_ref=att.at[s, r, :], dst_ref=att.at[s, r, :],
             send_sem=att_send.at[to, c], recv_sem=att_recv.at[s, c],
@@ -124,6 +136,9 @@
             meta_copy(d).start()
 
     gath[t] = res_ref[...]
+    top_s[...] = jnp.full(top_s.shape, -1e30, F32)
+    den_s[...] = jnp.zeros(den_s.shape, F32)
+    acc_s[...] = jnp.zeros(acc_s.shape, F32)
     mine = pl.ds(pl.multiple_of(g * wrows, wrows), wrows)
     wo_all[t, mine, :] = wo_ref[mine, pl.ds(pl.multiple_of(t * width, width), width)]
     for d in range(1, R + 1):
@@ -158,7 +173,61 @@
                     def _():
                         sib_copy(d, d + 1, c).start()
 
+    def wait_odd(c):
+        for d in range(1, R + 1, 2):
+            @pl.when(i >= d)
+            def _(d=d):
+                kv_copy(d, c).wait_recv()
+
+    def attend(a, c):
+        qr, kr = half_of(a), rows_of(c)
+        seg = seg_s[qr, :]
+        q_place = a * Q + lax.broadcasted_iota(jnp.int32, (Q, PAGE), 0)
+        k_place = c * PAGE + lax.broadcasted_iota(jnp.int32, (Q, PAGE), 1)
+        masks = []
+        for d in range(R + 1):
+            group = meta_ref[0:1, kr] if d == 0 else meta[d - 1, 0:1, kr]
+            allowed = group == seg
+            if d == 0:
+                allowed = allowed & (k_place <= q_place)
+            masks.append(jnp.where(allowed, 0.0, -1e30))
+        for h in range(HL):
+            cols = slice(h * 128, (h + 1) * 128)
+            q = qpad[qr, cols]
+            scores = []
+            most = None
+            for d in range(R + 1):
+                s = lax.dot_general(q, kv[d, kr, cols], (((1,), (1,)), ((), ())), preferred_element_type=F32) + masks[d]
+                scores.append(s)
+                most = s if most is None else jnp.maximum(most, s)
+            old = top_s[a, h]
+            top = jnp.maximum(old, jnp.max(most, axis=1, keepdims=True))
+            part = None
+            acc = None
+            for d in range(R + 1):
+                e = jnp.exp(scores[d] - top)
+                part = e if part is None else part + e
+                o = jnp.dot(e.astype(BF16), kv[d, kr, cols], preferred_element_type=F32)
+                acc = o if acc is None else acc + o
+            shrink = jnp.exp(old - top)
+            top_s[a, h] = top
+            den_s[a, h] = den_s[a, h] * shrink + jnp.sum(part, axis=1, keepdims=True)
+            acc_s[a, h] = acc_s[a, h] * shrink + acc
+
     def gather_step(c, carry):
+        r = rows_of(c)
+
+        def column(row):
+            return jnp.transpose(jnp.broadcast_to(row.astype(F32), (PAGE, 128)))
+
+        seg_col = column(meta_ref[12:13, r])
+        ok = column(meta_ref[13:14, r])
+        seg_s[r, :] = seg_col.astype(jnp.int32)
+        place = (i * rows_all + c * PAGE + lax.broadcasted_iota(jnp.int32, (PAGE, 128), 0)).astype(F32)
+        angles = (place - seg_col) * freq_ref[...]
+        cs = jnp.cos(angles)
+        sn = jnp.sin(angles)
+        sn = jnp.where(first, -sn, sn)
         for k in range(1, T):
             @pl.when(t - k >= 0)
             def _(k=k):
@@ -180,7 +249,11 @@
         def _():
             send_own(c + 2)
 
-        r = rows_of(c)
+        @pl.when(c == 0)
+        def _():
+            for load in loads:
+                load.wait()
+
         total = jnp.zeros((PAGE, 1), F32)
         for s in range(T):
             x = gath[s, r, :].astype(F32)
@@ -193,9 +266,6 @@
         n = nbuf[...]
         k_raw = jnp.dot(n, wk_ref[...], preferred_element_type=F32)
         v_raw = jnp.dot(n, wv_ref[...], preferred_element_type=F32)
-        cs = cos_ref[r, :]
-        sn = sin_ref[r, :]
-        ok = valid_ref[r, :]
         for pair in range(HL // 2):
             cols = slice(pair * 128, (pair + 1) * 128)
             kr = rotated(k_raw[:, cols], cs, sn) * ok
@@ -228,85 +298,79 @@
         @pl.when(c >= 1)
         def _():
             forward_kv(c - 1)
+
+        @pl.when(c == 2)
+        def _():
+            for d in range(1, R + 1):
+                @pl.when(i >= d)
+                def _(d=d):
+                    meta_copy(d).wait_recv()
+
+        @pl.when(c >= 2)
+        def _():
+            wait_odd(c - 2)
+            attend(0, c - 2)
         return carry
 
     lax.fori_loop(0, C, gather_step, 0)
-    forward_kv(C - 1)
-
-    for d in range(1, R + 1):
-        @pl.when(i >= d)
-        def _(d=d):
-            meta_copy(d).wait_recv()
-            if d % 2 == 1:
-                for c in range(C):
-                    kv_copy(d, c).wait_recv()
+
+    def attend_step(n, carry):
+        a = jnp.where(n < 2, 1, lax.rem(n, 2))
+        c = jnp.where(n < 2, n, n // 2 + 1)
+
+        @pl.when(n == 1)
+        def _():
+            forward_kv(C - 1)
+
+        @pl.when((n == 2) | (n == 4))
+        def _():
+            wait_odd(c)
+
+        attend(a, c)
+
+        @pl.when(n >= 4)
+        def _():
+            r = half_of(a)
+            low_q = lax.broadcasted_iota(jnp.int32, (Q, 128), 1) < HD
+            for pair in range(HL // 2):
+                one = acc_s[a, 2 * pair] / den_s[a, 2 * pair]
+                two = acc_s[a, 2 * pair + 1] / den_s[a, 2 * pair + 1]
+                both = jnp.where(low_q, pltpu.roll(one, HD, 1), two)
+                att[t, r, pair * 128:(pair + 1) * 128] = both.astype(BF16)
+            for k in range(1, T):
+                att_copy(t, lax.rem(t + k, T), a).start()
+        return carry
+
+    lax.fori_loop(0, 6, attend_step, 0)
+
+    slot_count = cache_ref.shape[0]
+
+    def cache_step(slot, carry):
+        page = jnp.zeros((PAGE, kv.shape[2]), BF16)
+        for b in range(2):
+            for p in range(C):
+                src = meta_ref[8 + p:9 + p, :] if b == 0 else meta[0, 8 + p:9 + p, :]
+                hit = jnp.where(src == i * slot_count + slot, 1.0, 0.0).astype(BF16)
+                page = page + kv[b, p * PAGE:(p + 1) * PAGE, :] * hit
+        cache_ref[slot] = page
+        return carry
+
+    lax.fori_loop(0, slot_count, cache_step, 0)
+
     for k in range(1, G):
         bc_copy(lax.rem(g + k, G), g).wait_recv()
 
-    keys = rows_all
-    slot_count = cache_ref.shape[0]
-
-    def attend_step(c, carry):
-        @pl.when(c < C)
-        def _():
-            r = rows_of(c)
-            seg = seg_ref[r, :][:, 0:1]
-            q_place = c * PAGE + lax.broadcasted_iota(jnp.int32, (PAGE, keys), 0)
-            k_place = lax.broadcasted_iota(jnp.int32, (PAGE, keys), 1)
-            for d in range(R + 1):
-                group = meta_ref[0:1, :] if d == 0 else meta[d - 1, 0:1, :]
-                allowed = group == seg
-                if d == 0:
-                    allowed = allowed & (k_place <= q_place)
-                bias[d] = jnp.where(allowed, 0.0, -1e30)
-            outs = []
-            for h in range(HL):
-                cols = slice(h * 128, (h + 1) * 128)
-                q = qpad[r, cols]
-                scores = []
-                top = None
-                for d in range(R + 1):
-                    s = lax.dot_general(q, kv[d, :, cols], (((1,), (1,)), ((), ())), preferred_element_type=F32) + bias[d]
-                    scores.append(s)
-                    here = jnp.max(s, axis=1, keepdims=True)
-                    top = here if top is None else jnp.maximum(top, here)
-                den = None
-                acc = None
-                for d in range(R + 1):
-                    e = jnp.exp(scores[d] - top)
-                    part = jnp.sum(e, axis=1, keepdims=True)
-                    den = part if den is None else den + part
-                    o = jnp.dot(e.astype(BF16), kv[d, :, cols], preferred_element_type=F32)
-                    acc = o if acc is None else acc + o
-                outs.append(acc / den)
-            for pair in range(HL // 2):
-                both = jnp.where(low, pltpu.roll(outs[2 * pair], HD, 1), outs[2 * pair + 1])
-                att[t, r, pair * 128:(pair + 1) * 128] = both.astype(BF16)
-            for k in range(1, T):
-                att_copy(t, lax.rem(t + k, T), c).start()
-            for j in range(slot_count // C):
-                slot = c * (slot_count // C) + j
-                page = jnp.zeros((PAGE, kv.shape[2]), BF16)
-                for b in range(2):
-                    for p in range(C):
-                        src = meta_ref[8 + p:9 + p, :] if b == 0 else meta[0, 8 + p:9 + p, :]
-                        hit = jnp.where(src == i * slot_count + slot, 1.0, 0.0).astype(BF16)
-                        page = page + kv[b, p * PAGE:(p + 1) * PAGE, :] * hit
-                cache_ref[slot] = page
-
-        @pl.when(c >= 1)
-        def _():
-            r = rows_of(c - 1)
-            for k in range(1, T):
-                att_copy(lax.rem(t + k, T), t, c - 1).wait_recv()
-            acc = res_ref[r, :].astype(F32)
-            proj = jnp.dot(att[0, r, :], wo_all[0], preferred_element_type=F32)
-            for s in range(1, T):
-                proj = proj + jnp.dot(att[s, r, :], wo_all[s], preferred_element_type=F32)
-            hid_ref[r, :] = (acc + proj).astype(BF16)
+    def project_step(a, carry):
+        r = half_of(a)
+        for k in range(1, T):
+            att_copy(lax.rem(t + k, T), t, a).wait_recv()
+        proj = jnp.dot(att[0, r, :], wo_all[0], preferred_element_type=F32)
+        for s in range(1, T):
+            proj = proj + jnp.dot(att[s, r, :], wo_all[s], preferred_element_type=F32)
+        hid_ref[r, :] = (res_ref[r, :].astype(F32) + proj).astype(BF16)
         return carry
 
-    lax.fori_loop(0, C + 1, attend_step, 0)
+    lax.fori_loop(0, 2, project_step, 0)
 
     for k in range(1, T):
         wo_copy(t, lax.rem(t + k, T)).wait_send()
@@ -345,11 +409,12 @@
         @pl.when(core == 0)
         def _():
             sib_copy(0, 1, c).wait_send()
+        return carry
+
+    lax.fori_loop(0, C, drain, 0)
+    for a in range(2):
         for k in range(1, T):
-            att_copy(t, lax.rem(t + k, T), c).wait_send()
-        return carry
-
-    lax.fori_loop(0, C, drain, 0)
+            att_copy(t, lax.rem(t + k, T), a).wait_send()
 
 
 def body(
@@ -364,21 +429,15 @@
     pages = page_slot.shape[0]
     slot_count = 2 * pages
     kvw = local_heads * 2 * HD
-    first_row = lax.axis_index("seq") * rows
-    offset = (first_row + jnp.arange(rows, dtype=jnp.int32) - segment_start).astype(F32)
     frequency = THETA ** (-2.0 * jnp.arange(HD // 2, dtype=F32) / HD)
-    angles = offset[:, None] * frequency[None, :]
-    cosine = jnp.cos(angles)
-    sine = jnp.sin(angles)
-    cos_t = jnp.concatenate([cosine] * 4, axis=1)
-    sin_t = jnp.concatenate([-sine, sine, -sine, sine], axis=1)
-    seg_t = jnp.broadcast_to(segment_start[:, None], (rows, 128))
-    valid_t = jnp.broadcast_to((token_valid > 0).astype(F32)[:, None], (rows, 128))
+    freq_t = jnp.concatenate([frequency] * 4)[None, :]
     group = jnp.where(token_valid > 0, segment_start, -1)
     meta_t = jnp.concatenate([
         jnp.broadcast_to(group[None, :], (8, rows)),
         jnp.broadcast_to(page_slot[:, None], (pages, rows)),
-        jnp.full((8 - pages, rows), -1, jnp.int32),
+        segment_start[None, :],
+        (token_valid > 0).astype(jnp.int32)[None, :],
+        jnp.full((6 - pages, rows), -1, jnp.int32),
     ], axis=0)
     dma = pltpu.SemaphoreType.DMA
     vmem = pl.BlockSpec(memory_space=pltpu.VMEM)
@@ -388,7 +447,7 @@
             jax.ShapeDtypeStruct((rows, width), BF16),
             jax.ShapeDtypeStruct((slot_count, PAGE, kvw), BF16),
         ),
-        in_specs=[vmem] * 11,
+        in_specs=[vmem] * 3 + [pl.BlockSpec(memory_space=pl.ANY)] * 3 + [vmem] * 2,
         out_specs=(vmem, vmem),
         scratch_shapes=[
             pltpu.VMEM((T, rows, width), BF16),
@@ -398,17 +457,23 @@
             pltpu.VMEM((R, 16, rows), jnp.int32),
             pltpu.VMEM((T, rows, local_heads * HD), BF16),
             pltpu.VMEM((T, local_heads * HD, width), BF16),
-            pltpu.VMEM((R + 1, PAGE, rows), F32),
+            pltpu.VMEM((rows, 128), jnp.int32),
+            pltpu.VMEM((2, local_heads, rows // 2, 1), F32),
+            pltpu.VMEM((2, local_heads, rows // 2, 1), F32),
+            pltpu.VMEM((2, local_heads, rows // 2, 128), F32),
+            pltpu.VMEM(query_weight.shape, BF16),
+            pltpu.VMEM(query_weight.shape, BF16),
+            pltpu.VMEM(query_weight.shape, BF16),
+            dma((3,)),
             dma((T, C)), dma((T, C)), dma((T, C)),
             dma((T,)), dma((T,)), dma((G,)), dma((G,)), dma((R,)), dma((R,)),
-            dma((R + 1, C)), dma((R + 1, C)), dma((R + 1, C)), dma((T, C)), dma((T, C)),
+            dma((R + 1, C)), dma((R + 1, C)), dma((R + 1, C)), dma((T, 2)), dma((T, 2)),
         ],
         compiler_params=pltpu.CompilerParams(
             collective_id=0, has_side_effects=True, vmem_limit_bytes=56 * 1024 * 1024
         ),
         cost_estimate=pl.CostEstimate(flops=4 * 10**9, bytes_accessed=8 * 10**6, transcendentals=5 * 10**6),
-    )(residual, norm_gain[None, :], query_weight, key_weight, value_weight, out_weight,
-      cos_t, sin_t, seg_t, valid_t, meta_t)
+    )(residual, norm_gain[None, :], freq_t, query_weight, key_weight, value_weight, out_weight, meta_t)
     return hidden, cache
 
 

time: 100 us -> 98.1 us (0.981)
  the two profiles are of different devices: /device:TPU:15 before, /device:TPU:12 now
where the time goes in v2:
time: 98.1 us; the launch traced here: 97.9 us
  Pallas kernels  91 us (93%)
  local copies, waits for them, and re-layouts  5.63 us (6%)
    pallas_call x1, Pallas kernels, body(): pl.pallas_call(functools.partial(kernel, S, T, R, G), out_shape=(jax.Shap...  91 us
    unnamed x10, local copies, waits for them, and re-layouts  4.33 us

profile of v2, /device:TPU:12, one launch (start us, length us, event | category | flops | bytes accessed | tf_op | source)
XLA Modules:
  0.0 97.9 jit_solution(6098166587370007393)
XLA Ops:
  0.6 0.0 copy-start.2
  0.7 0.6 maximum_bitcast_fusion.freq_ref
  1.2 0.1 copy-done.2
  1.3 0.0 copy-start.1
  1.3 0.7 copy-done.1
  2.0 0.0 copy-start.3
  2.0 0.6 copy-done.3
  2.7 0.1 broadcast_in_dim.38
  2.7 1.2 %concatenate.7.meta_ref = s32[16,512]{1,0:T(8,128)} concatenate(s32[8,512]{1,0:T(8,128)S(1)} %broadcast_in_dim.37, s32[4,512]{1,0:T(4,128)S(1)} %broadcast_in_dim.38, s32[1,512]{1,0:T(1,128)S(1)} %bitcast.5, s32[1,512]{1,0:T(1,128)S(1)} %bitcast.6, s32[2,512]{1,0:T(2,128)S(1)} %broadcast_in_dim.42), dimensions={0} | concatenate | bytes 65536 | tf_op jit(solution)/shard_map/concatenate | solution.py:435
  4.0 91.0 %shard_map.104 = (bf16[512,512]{1,0:T(8,128)(2,1)}, bf16[8,128,512]{2,1,0:T(8,128)(2,1)}) custom-call(bf16[512,512]{1,0:T(8,128)(2,1)} %res_ref.1, f32[1,2048]{1,0:T(1,128)} %bitcast.7, f32[1,128]{1,0:T(1,128)} %maximum_bitcast_fusion.freq_ref, bf16[2048,256]{1,0:T(8,128)(2,1)} %wq_hbm.1, bf16[2048,256]{1,0:T(8,128)(2,1)} %wk_hbm.1, ...), custom_call_target="tpu_custom_call" | custom-call | flops 4000000000 | bytes 8000000 | tf_op jit(solution)/shard_map/pallas_call | solution.py:444
  94.9 0.0 copy-start
  94.9 2.0 %copy.13 = bf16[512,512]{1,0:T(8,128)(2,1)} copy(bf16[512,512]{1,0:T(8,128)(2,1)} %get-tuple-element.6) | data formatting | bytes 1048576
  96.9 0.0 copy-done
  96.9 1.0 copy.14
  (5 shorter events, 0.0 us)
Async XLA Ops:
  0.6 0.7 copy-start.2
  1.3 0.7 copy-start.1
  2.0 0.7 copy-start.3
  94.9 2.0 %copy-start = (bf16[8,128,512]{2,1,0:T(8,128)(2,1)S(1)}, bf16[8,128,512]{2,1,0:T(8,128)(2,1)}, u32[]{:S(2)}) copy-start(bf16[8,128,512]{2,1,0:T(8,128)(2,1)} %get-tuple-element.7) | copy-start | bytes 3145732

commit v3 on v2

--- a/solution.py
+++ b/solution.py
@@ -126,8 +126,6 @@
             z_copy(t, c, -1, True).start()
 
     send_own(0)
-    for k in range(1, T):
-        wo_copy(t, lax.rem(t + k, T)).start()
     if C > 1:
         send_own(1)
     for d in range(1, R + 1):
@@ -288,43 +286,46 @@
             qpad[r, pair * 256:pair * 256 + 128] = jnp.where(low, qr, 0.0).astype(BF16)
             qpad[r, pair * 256 + 128:pair * 256 + 256] = jnp.where(low, pltpu.roll(qr, HD, 1), 0.0).astype(BF16)
 
-        @pl.when(c == 0)
+        @pl.when(c >= 1)
+        def _():
+            forward_kv(c - 1)
+
+        @pl.when(c == 2)
+        def _():
+            for d in range(1, R + 1):
+                @pl.when(i >= d)
+                def _(d=d):
+                    meta_copy(d).wait_recv()
+
+        @pl.when(c >= 2)
+        def _():
+            wait_odd(c - 2)
+            attend(0, c - 2)
+        return carry
+
+    lax.fori_loop(0, C, gather_step, 0)
+
+    for k in range(1, T):
+        wo_copy(t, lax.rem(t + k, T)).start()
+
+    def attend_step(n, carry):
+        a = jnp.where(n < 2, 1, lax.rem(n, 2))
+        c = jnp.where(n < 2, n, n // 2 + 1)
+
+        @pl.when(n == 1)
+        def _():
+            forward_kv(C - 1)
+
+        @pl.when((n == 2) | (n == 4))
+        def _():
+            wait_odd(c)
+
+        @pl.when(n == 4)
         def _():
             for k in range(1, T):
                 wo_copy(lax.rem(t + k, T), t).wait_recv()
             for k in range(1, G):
                 bc_copy(g, lax.rem(g + k, G)).start()
-
-        @pl.when(c >= 1)
-        def _():
-            forward_kv(c - 1)
-
-        @pl.when(c == 2)
-        def _():
-            for d in range(1, R + 1):
-                @pl.when(i >= d)
-                def _(d=d):
-                    meta_copy(d).wait_recv()
-
-        @pl.when(c >= 2)
-        def _():
-            wait_odd(c - 2)
-            attend(0, c - 2)
-        return carry
-
-    lax.fori_loop(0, C, gather_step, 0)
-
-    def attend_step(n, carry):
-        a = jnp.where(n < 2, 1, lax.rem(n, 2))
-        c = jnp.where(n < 2, n, n // 2 + 1)
-
-        @pl.when(n == 1)
-        def _():
-            forward_kv(C - 1)
-
-        @pl.when((n == 2) | (n == 4))
-        def _():
-            wait_odd(c)
 
         attend(a, c)
 

time: 98.1 us -> 83.6 us (0.85)
  the two profiles are of different devices: /device:TPU:12 before, /device:TPU:0 now
where the time goes in v3:
time: 83.6 us; the launch traced here: 83.4 us
  Pallas kernels  76.5 us (92%)
  local copies, waits for them, and re-layouts  5.63 us (7%)
    pallas_call x1, Pallas kernels, body(): pl.pallas_call(functools.partial(kernel, S, T, R, G), out_shape=(jax.Shap...  76.5 us
    unnamed x10, local copies, waits for them, and re-layouts  4.33 us

profile of v3, /device:TPU:0, one launch (start us, length us, event | category | flops | bytes accessed | tf_op | source)
XLA Modules:
  0.0 83.4 jit_solution(12420398399185945310)
XLA Ops:
  0.6 0.0 copy-start.2
  0.7 0.6 maximum_bitcast_fusion.freq_ref
  1.2 0.1 copy-done.2
  1.3 0.0 copy-start.1
  1.3 0.7 copy-done.1
  2.0 0.0 copy-start.3
  2.0 0.6 copy-done.3
  2.7 0.1 broadcast_in_dim.38
  2.7 1.2 %concatenate.7.meta_ref = s32[16,512]{1,0:T(8,128)} concatenate(s32[8,512]{1,0:T(8,128)S(1)} %broadcast_in_dim.37, s32[4,512]{1,0:T(4,128)S(1)} %broadcast_in_dim.38, s32[1,512]{1,0:T(1,128)S(1)} %bitcast.5, s32[1,512]{1,0:T(1,128)S(1)} %bitcast.6, s32[2,512]{1,0:T(2,128)S(1)} %broadcast_in_dim.42), dimensions={0} | concatenate | bytes 65536 | tf_op jit(solution)/shard_map/concatenate | solution.py:436
  4.0 76.5 %shard_map.104 = (bf16[512,512]{1,0:T(8,128)(2,1)}, bf16[8,128,512]{2,1,0:T(8,128)(2,1)}) custom-call(bf16[512,512]{1,0:T(8,128)(2,1)} %res_ref.1, f32[1,2048]{1,0:T(1,128)} %bitcast.7, f32[1,128]{1,0:T(1,128)} %maximum_bitcast_fusion.freq_ref, bf16[2048,256]{1,0:T(8,128)(2,1)} %wq_hbm.1, bf16[2048,256]{1,0:T(8,128)(2,1)} %wk_hbm.1, ...), custom_call_target="tpu_custom_call" | custom-call | flops 4000000000 | bytes 8000000 | tf_op jit(solution)/shard_map/pallas_call | solution.py:445
  80.4 0.0 copy-start
  80.4 2.0 %copy.13 = bf16[512,512]{1,0:T(8,128)(2,1)} copy(bf16[512,512]{1,0:T(8,128)(2,1)} %get-tuple-element.6) | data formatting | bytes 1048576
  82.4 0.0 copy-done
  82.4 1.0 %copy.14 = bf16[8,128,512]{2,1,0:T(8,128)(2,1)} copy(bf16[8,128,512]{2,1,0:T(8,128)(2,1)S(1)} %copy-done) | data formatting | bytes 2097152
  (5 shorter events, 0.0 us)
Async XLA Ops:
  0.6 0.7 copy-start.2
  1.3 0.7 copy-start.1
  2.0 0.7 copy-start.3
  80.4 2.0 %copy-start = (bf16[8,128,512]{2,1,0:T(8,128)(2,1)S(1)}, bf16[8,128,512]{2,1,0:T(8,128)(2,1)}, u32[]{:S(2)}) copy-start(bf16[8,128,512]{2,1,0:T(8,128)(2,1)} %get-tuple-element.7) | copy-start | bytes 3145732
